TPU v7x, 32 devices: a whole 2x2x4 slice. The times are simulated.
32 devices in a mesh: grp: 2 (over core), dp: 16 (over z, y, x).
Axes of the slice: x: 2, y: 2, z: 4, core: 2. Of those that a mesh axis runs over, the one named last changes fastest.
Arguments:
- question_ids: int32 [512, 64], P(('grp', 'dp')), may hold values from 0 to 30719
- passage_ids: int32 [1024, 256], P(('grp', 'dp')), may hold values from 0 to 30719
- question_lengths: int32 [512], P(('grp', 'dp')), may hold values from 16 to 64
- passage_lengths: int32 [1024], P(('grp', 'dp')), may hold values from 64 to 256
- question_keys: int32 [512], P(('grp', 'dp')), may hold values from 0 to 15
- passage_keys: int32 [1024], P(('grp', 'dp')), may hold values from 0 to 15
- question_valid: int32 [512], P(('grp', 'dp')), may hold values 0 or 1
- word_table: float32 [2, 30720, 128], P('grp', 'dp'), may hold values from -0.3125 to 0.3125
- positions: float32 [2, 2, 256, 128], P('grp'), may hold values from -0.3125 to 0.3125
- attention: float32 [2, 2, 128, 512], P('grp'), may hold values from -0.5 to 0.5
- feedforward: float32 [2, 2, 2, 128, 512], P('grp'), may hold values from -0.5 to 0.5
- vectors: float32 [2, 2, 14, 128], P('grp'), as said below
- word_first: float32 [2, 30720, 128], P('grp', 'dp'), may hold values from -8.940697e-08 to 8.940697e-08
- positions_first: float32 [2, 2, 256, 128], P('grp'), may hold values from -3.33786e-06 to 3.33786e-06
- attention_first: float32 [2, 2, 128, 512], P('grp'), may hold values from -3.33786e-06 to 3.33786e-06
- feedforward_first: float32 [2, 2, 2, 128, 512], P('grp'), may hold values from -3.33786e-06 to 3.33786e-06
- vectors_first: float32 [2, 2, 14, 128], P('grp'), may hold values from -1.335144e-05 to 1.335144e-05
- word_second: float32 [2, 30720, 128], P('grp', 'dp'), may hold values from 1.0240082e-15 to 1.6384131e-14
- positions_second: float32 [2, 2, 256, 128], P('grp'), may hold values from 1.1377869e-14 to 1.820459e-13
- attention_second: float32 [2, 2, 128, 512], P('grp'), may hold values from 1.1377869e-14 to 1.820459e-13
- feedforward_second: float32 [2, 2, 2, 128, 512], P('grp'), may hold values from 1.1377869e-14 to 1.820459e-13
- vectors_second: float32 [2, 2, 14, 128], P('grp'), may hold values from 1.820459e-13 to 2.9127345e-12
- word_anchor: float32 [30720, 128], P('dp'), may hold values from -0.3125 to 0.3125
- positions_anchor: float32 [2, 256, 128], replicated, may hold values from -0.3125 to 0.3125
- attention_anchor: float32 [2, 128, 512], replicated, may hold values from -0.5 to 0.5
- feedforward_anchor: float32 [2, 2, 128, 512], replicated, may hold values from -0.5 to 0.5
- vectors_anchor: float32 [2, 14, 128], replicated, as said below
- word_outer: float32 [30720, 128], P('dp'), may hold values from -0.3125 to 0.3125
- positions_outer: float32 [2, 256, 128], replicated, may hold values from -0.3125 to 0.3125
- attention_outer: float32 [2, 128, 512], replicated, may hold values from -0.3125 to 0.3125
- feedforward_outer: float32 [2, 2, 128, 512], replicated, may hold values from -0.3125 to 0.3125
- vectors_outer: float32 [2, 14, 128], replicated, may hold values from -1.25 to 1.25
Outputs:
- loss_sum: float32 [2], P('grp')
- loss_count: float32 [2], P('grp')
- grad_norm: float32 [2], P('grp')
- word_first_next: float32 [2, 30720, 128], P('grp', 'dp')
- positions_first_next: float32 [2, 2, 256, 128], P('grp')
- attention_first_next: float32 [2, 2, 128, 512], P('grp')
- feedforward_first_next: float32 [2, 2, 2, 128, 512], P('grp')
- vectors_first_next: float32 [2, 2, 14, 128], P('grp')
- word_second_next: float32 [2, 30720, 128], P('grp', 'dp')
- positions_second_next: float32 [2, 2, 256, 128], P('grp')
- attention_second_next: float32 [2, 2, 128, 512], P('grp')
- feedforward_second_next: float32 [2, 2, 2, 128, 512], P('grp')
- vectors_second_next: float32 [2, 2, 14, 128], P('grp')
- word_average: float32 [30720, 128], P('dp')
- positions_average: float32 [2, 256, 128], replicated
- attention_average: float32 [2, 128, 512], replicated
- feedforward_average: float32 [2, 2, 128, 512], replicated
- vectors_average: float32 [2, 14, 128], replicated
- word_outer_next: float32 [30720, 128], P('dp')
- positions_outer_next: float32 [2, 256, 128], replicated
- attention_outer_next: float32 [2, 128, 512], replicated
- feedforward_outer_next: float32 [2, 2, 128, 512], replicated
- vectors_outer_next: float32 [2, 14, 128], replicated
- word_weight_next: float32 [2, 30720, 128], P('grp', 'dp')
- positions_weight_next: float32 [2, 2, 256, 128], P('grp')
- attention_weight_next: float32 [2, 2, 128, 512], P('grp')
- feedforward_weight_next: float32 [2, 2, 2, 128, 512], P('grp')
- vectors_weight_next: float32 [2, 2, 14, 128], P('grp')
Inputs may be any that keep to these rules, and one draw needn't show every extreme that they name: `vectors`: rows 0, 5 and 8 are norm gains near one, the others biases. `vectors_anchor`: rows 0, 5 and 8 are norm gains near one, the others biases.
All inputs are finite; a program needn't handle non-finite values. No bound on the sum of `question_valid` on one device may be relied on, other than what follows from the above.
Results may differ from a plain program's by a relative error of at most 0.018.
The roundings to bfloat16 on the way count: a program that leaves them out, or rounds other values in their place, can miss the bound.
Values may be sent and summed in bfloat16 or wider, within the bound.
A program may use at most 256 MiB of HBM per device.

v0:
```python
import jax
import jax.numpy as jnp
from jax import lax
from jax.sharding import PartitionSpec as P

HEAD = 64
STEP = 5


NORM_EPS = 1e-05
MASKED = -1000000000.0
BETA_ONE = 0.9
BETA_TWO = 0.999
INNER_RATE = 0.05
WEIGHT_DECAY = 0.01
ADAM_EPS = 1e-08
CLIP_LIMIT = 0.01
OUTER_RATE = 0.7
OUTER_MU = 0.9
CONTRACT_ROWS = (((0,), (0,)), ((), ()))
CONTRACT_LAST = (((1,), (1,)), ((), ()))


def layer_norm(values, gain, shift):
    center = values - jnp.mean(values, -1, keepdims=True)
    spread = jnp.mean(center * center, -1, keepdims=True)
    return center * lax.rsqrt(spread + NORM_EPS) * gain + shift


def gelu_tanh(values):
    return jax.nn.gelu(values, approximate=True)


def low16(values):
    return values.astype(jnp.bfloat16)


def attention_scores(query, keys_all, lengths):
    scores = jnp.einsum(
        "bqhe,bkhe->bhqk", query, keys_all, preferred_element_type=jnp.float32
    ) * HEAD ** (-0.5)
    keep = jnp.arange(query.shape[1])[None, None, None, :] < lengths[:, None, None, None]
    return jnp.where(keep, scores, MASKED)


def prepare(positions, attention, feedforward, vectors, encoder):
    weights = (
        positions[0, encoder],
        attention[0, encoder],
        feedforward[0, encoder],
        vectors[0, encoder],
    )
    width = attention.shape[2]
    attn_w = weights[1]
    ffn_w = weights[2]
    low_weights = (
        low16(attn_w[:, : 3 * width]),
        low16(attn_w[:, 3 * width :]),
        low16(ffn_w[0]),
        low16(ffn_w[1]),
    )
    return (weights, low_weights)


def forward(wide, weights, low_weights, token_ids, lengths):
    place, attn_w, ffn_w, vec = weights
    w_qkv, w_out, w_up, w_down = low_weights
    sequences, seq = token_ids.shape
    width = attn_w.shape[0]
    heads = width // HEAD
    x_embed = jnp.take(wide, token_ids, axis=0).astype(jnp.float32) + place[:seq]
    h_embed = layer_norm(x_embed, vec[0], vec[1])
    a_low = low16(h_embed)
    bias_row = jnp.concatenate([vec[2], jnp.zeros_like(vec[2]), vec[3]])
    qkv = low16(
        jnp.einsum("bld,de->ble", a_low, w_qkv, preferred_element_type=jnp.float32) + bias_row
    )
    split = qkv.reshape(sequences, seq, 3, heads, HEAD)
    scores = attention_scores(split[:, :, 0], split[:, :, 1], lengths)
    top = jnp.max(scores, -1, keepdims=True)
    expo = jnp.exp(scores - top)
    total = jnp.sum(expo, -1, keepdims=True)
    probs = expo / total
    lse = top + jnp.log(total)
    mixed = jnp.einsum(
        "bhqk,bkhe->bqhe", low16(probs), split[:, :, 2], preferred_element_type=jnp.float32
    )
    mixed = low16(mixed.reshape(sequences, seq, width))
    x_attn = h_embed + (
        jnp.einsum("bld,de->ble", mixed, w_out, preferred_element_type=jnp.float32) + vec[4]
    )
    h_attn = layer_norm(x_attn, vec[5], vec[6])
    h_low = low16(h_attn)
    pre = jnp.einsum("bld,df->blf", h_low, w_up, preferred_element_type=jnp.float32) + vec[
        10:
    ].reshape(-1)
    act = low16(gelu_tanh(pre))
    x_ffn = h_attn + (
        jnp.einsum("blf,df->bld", act, w_down, preferred_element_type=jnp.float32) + vec[7]
    )
    h_out = layer_norm(x_ffn, vec[8], vec[9])
    kept = (x_embed, x_attn, x_ffn, a_low, qkv, lse, mixed, h_low, pre, act)
    return (h_out[:, 0], kept)


def backward(weights, low_weights, lengths, kept, d_cls):
    place, attn_w, ffn_w, vec = weights
    w_qkv, w_out, w_up, w_down = low_weights
    x_embed, x_attn, x_ffn, a_low, qkv, lse, mixed, h_low, pre, act = kept
    sequences, seq, width = x_embed.shape
    heads = width // HEAD
    d_top = jnp.zeros_like(x_ffn).at[:, 0].set(d_cls)
    unused, out_back = jax.vjp(layer_norm, x_ffn, vec[8], vec[9])
    d_x_ffn, d_gain_two, d_shift_two = out_back(d_top)
    d_branch = low16(d_x_ffn)
    d_down_bias = jnp.sum(d_branch, (0, 1), dtype=jnp.float32)
    d_down = jnp.einsum("bld,blf->df", d_branch, act, preferred_element_type=jnp.float32)
    d_act = jnp.einsum("bld,df->blf", d_branch, w_down, preferred_element_type=jnp.float32)
    unused, gelu_back = jax.vjp(gelu_tanh, pre)
    d_pre = low16(gelu_back(d_act)[0])
    d_up_bias = jnp.sum(d_pre, (0, 1), dtype=jnp.float32)
    d_up = jnp.einsum("bld,blf->df", h_low, d_pre, preferred_element_type=jnp.float32)
    d_h_attn = d_x_ffn + jnp.einsum("blf,df->bld", d_pre, w_up, preferred_element_type=jnp.float32)
    unused, attn_back = jax.vjp(layer_norm, x_attn, vec[5], vec[6])
    d_x_attn, d_gain_one, d_shift_one = attn_back(d_h_attn)
    d_proj = low16(d_x_attn)
    d_out_bias = jnp.sum(d_proj, (0, 1), dtype=jnp.float32)
    d_w_out = jnp.einsum("bld,ble->de", mixed, d_proj, preferred_element_type=jnp.float32)
    d_mixed = low16(jnp.einsum("ble,de->bld", d_proj, w_out, preferred_element_type=jnp.float32))
    d_mixed = d_mixed.reshape(sequences, seq, heads, HEAD)
    split = qkv.reshape(sequences, seq, 3, heads, HEAD)
    query, keys_all, values_all = (split[:, :, 0], split[:, :, 1], split[:, :, 2])
    probs = jnp.exp(attention_scores(query, keys_all, lengths) - lse)
    d_probs = jnp.einsum("bqhe,bkhe->bhqk", d_mixed, values_all, preferred_element_type=jnp.float32)
    d_values = jnp.einsum(
        "bhqk,bqhe->bkhe", low16(probs), d_mixed, preferred_element_type=jnp.float32
    )
    d_scores = low16(probs * (d_probs - jnp.sum(probs * d_probs, -1, keepdims=True)))
    d_query = jnp.einsum(
        "bhqk,bkhe->bqhe", d_scores, keys_all, preferred_element_type=jnp.float32
    ) * HEAD ** (-0.5)
    d_keys = jnp.einsum(
        "bhqk,bqhe->bkhe", d_scores, query, preferred_element_type=jnp.float32
    ) * HEAD ** (-0.5)
    d_qkv = low16(jnp.stack([d_query, d_keys, d_values], 2).reshape(sequences, seq, 3 * width))
    bias_sum = jnp.sum(d_qkv, (0, 1), dtype=jnp.float32)
    d_w_qkv = jnp.einsum("bld,ble->de", a_low, d_qkv, preferred_element_type=jnp.float32)
    d_h_embed = d_x_attn + jnp.einsum(
        "ble,de->bld", d_qkv, w_qkv, preferred_element_type=jnp.float32
    )
    unused, embed_back = jax.vjp(layer_norm, x_embed, vec[0], vec[1])
    d_x_embed, d_gain_embed, d_shift_embed = embed_back(d_h_embed)
    d_place = jnp.zeros_like(place).at[:seq].set(jnp.sum(d_x_embed, 0))
    d_attn = jnp.concatenate([d_w_qkv, d_w_out], 1)
    d_ffn = jnp.stack([d_up, d_down])
    d_rows = jnp.stack(
        [
            d_gain_embed,
            d_shift_embed,
            bias_sum[:width],
            bias_sum[2 * width :],
            d_out_bias,
            d_gain_one,
            d_shift_one,
            d_down_bias,
            d_gain_two,
            d_shift_two,
        ]
    )
    d_vec = jnp.concatenate([d_rows, d_up_bias.reshape(-1, width)])
    return ((d_place, d_attn, d_ffn, d_vec), d_x_embed)


def softmax_terms(scores, drop, target, weight, count):
    masked = jnp.where(drop, MASKED, scores)
    top = jnp.max(masked, -1, keepdims=True)
    expo = jnp.exp(masked - top)
    total = jnp.sum(expo, -1, keepdims=True)
    lse = (top + jnp.log(total))[:, 0]
    picked = jnp.sum(jnp.where(target, scores, 0.0), -1)
    loss_rows = weight * (lse - picked)
    grad = low16((weight / count)[:, None] * (expo / total - target.astype(jnp.float32)))
    return (grad, loss_rows)


def directions(
    rows_q,
    rows_p,
    every_q,
    every_p,
    row_keys_q,
    row_keys_p,
    row_valid,
    keys_q,
    keys_p,
    valid_q,
    first_q,
    first_p,
    count,
):
    scale = rows_q.shape[1] ** (-0.5)
    index_q = jnp.arange(every_q.shape[0])
    index_p = jnp.arange(every_p.shape[0])
    global_q = first_q + jnp.arange(rows_q.shape[0])
    global_p = first_p + jnp.arange(rows_p.shape[0])
    scores_qp = (
        lax.dot_general(rows_q, every_p, CONTRACT_LAST, preferred_element_type=jnp.float32) * scale
    )
    target_qp = index_p[None, :] == 2 * global_q[:, None]
    drop_qp = (row_keys_q[:, None] == keys_p[None, :]) & ~target_qp
    grad_qp, loss_qp = softmax_terms(
        scores_qp, drop_qp, target_qp, row_valid.astype(jnp.float32), count
    )
    scores_pq = (
        lax.dot_general(rows_p, every_q, CONTRACT_LAST, preferred_element_type=jnp.float32) * scale
    )
    owner = global_p // 2
    target_pq = index_q[None, :] == owner[:, None]
    drop_pq = ((row_keys_p[:, None] == keys_q[None, :]) | (valid_q[None, :] == 0)) & ~target_pq
    owner_valid = jnp.sum(jnp.where(target_pq, valid_q[None, :], 0), 1)
    weight_p = jnp.where(global_p % 2 == 0, owner_valid, 0).astype(jnp.float32)
    grad_pq, loss_pq = softmax_terms(scores_pq, drop_pq, target_pq, weight_p, count)
    return (grad_qp, grad_pq, loss_qp, loss_pq)


def adam(weight, grad, first, second):
    first_new = BETA_ONE * first + (1.0 - BETA_ONE) * grad
    second_new = BETA_TWO * second + (1.0 - BETA_TWO) * grad * grad
    fix_one = 1.0 - BETA_ONE**STEP
    fix_two = 1.0 - BETA_TWO**STEP
    ratio = first_new / fix_one / (jnp.sqrt(second_new / fix_two) + ADAM_EPS)
    return (first_new, second_new, weight - INNER_RATE * (ratio + WEIGHT_DECAY * weight))


def body(
    question_ids,
    passage_ids,
    question_lengths,
    passage_lengths,
    question_keys,
    passage_keys,
    question_valid,
    word_table,
    positions,
    attention,
    feedforward,
    vectors,
    word_first,
    positions_first,
    attention_first,
    feedforward_first,
    vectors_first,
    word_second,
    positions_second,
    attention_second,
    feedforward_second,
    vectors_second,
    word_anchor,
    positions_anchor,
    attention_anchor,
    feedforward_anchor,
    vectors_anchor,
    word_outer,
    positions_outer,
    attention_outer,
    feedforward_outer,
    vectors_outer,
):
    wide = lax.all_gather(low16(word_table[0]), "dp", axis=0, tiled=True)
    question_weights, question_lows = prepare(positions, attention, feedforward, vectors, 0)
    passage_weights, passage_lows = prepare(positions, attention, feedforward, vectors, 1)
    cls_question, kept_question = forward(
        wide, question_weights, question_lows, question_ids, question_lengths
    )
    cls_passage, kept_passage = forward(
        wide, passage_weights, passage_lows, passage_ids, passage_lengths
    )
    own_q = low16(cls_question)
    own_p = low16(cls_passage)
    every_q, every_p = (
        lax.all_gather(own_q, "dp", axis=0, tiled=True),
        lax.all_gather(own_p, "dp", axis=0, tiled=True),
    )
    keys_q, keys_p, valid_all = (
        lax.all_gather(question_keys, "dp", axis=0, tiled=True),
        lax.all_gather(passage_keys, "dp", axis=0, tiled=True),
        lax.all_gather(question_valid, "dp", axis=0, tiled=True),
    )
    count = jnp.maximum(jnp.sum(valid_all).astype(jnp.float32), 1.0)
    device = lax.axis_index("dp")
    local_q = question_ids.shape[0]
    local_p = passage_ids.shape[0]
    grad_qp, grad_pq, loss_qp, loss_pq = directions(
        own_q,
        own_p,
        every_q,
        every_p,
        question_keys,
        passage_keys,
        question_valid,
        keys_q,
        keys_p,
        valid_all,
        device * local_q,
        device * local_p,
        count,
    )
    rows_each = local_q + local_p
    many = lax.axis_size("dp") * rows_each // rows_each
    part_q = lax.dot_general(grad_pq, own_p, CONTRACT_ROWS, preferred_element_type=jnp.float32)
    part_p = lax.dot_general(grad_qp, own_q, CONTRACT_ROWS, preferred_element_type=jnp.float32)
    joined = jnp.concatenate(
        [part_q.reshape(many, local_q, -1), part_p.reshape(many, local_p, -1)], 1
    )
    received = lax.psum_scatter(
        joined.reshape(many * rows_each, -1), "dp", scatter_dimension=0, tiled=True
    )
    d_cls_q = jnp.dot(grad_qp, every_p, preferred_element_type=jnp.float32) + received[:local_q]
    d_cls_p = jnp.dot(grad_pq, every_q, preferred_element_type=jnp.float32) + received[local_q:]
    loss_local = jnp.sum(loss_qp) + jnp.sum(loss_pq)
    loss_total = lax.psum(loss_local, "dp")
    scale = every_q.shape[1] ** (-0.5)
    grads_q, embed_q = backward(
        question_weights, question_lows, question_lengths, kept_question, d_cls_q * scale
    )
    grads_p, embed_p = backward(
        passage_weights, passage_lows, passage_lengths, kept_passage, d_cls_p * scale
    )
    width = embed_q.shape[-1]
    token_ids = jnp.concatenate([question_ids.reshape(-1), passage_ids.reshape(-1)])
    token_grads = jnp.concatenate([embed_q.reshape(-1, width), embed_p.reshape(-1, width)])
    table_full = jax.ops.segment_sum(token_grads, token_ids, num_segments=wide.shape[0])
    table_grad = lax.psum_scatter(table_full, "dp", scatter_dimension=0, tiled=True)
    stacked = tuple((jnp.stack([left, right]) for left, right in zip(grads_q, grads_p)))
    place_grad, attn_grad, ffn_grad, vec_grad = lax.psum(
        (stacked[0], stacked[1], stacked[2], stacked[3]), "dp"
    )
    table_local_sq = jnp.sum(table_grad * table_grad)
    table_sq = lax.psum(table_local_sq, "dp")
    grads = (table_grad[None], place_grad[None], attn_grad[None], ffn_grad[None], vec_grad[None])
    norm = jnp.sqrt(table_sq + sum((jnp.sum(g * g) for g in grads[1:])))
    factor = CLIP_LIMIT / jnp.maximum(norm, CLIP_LIMIT)
    weights = (word_table, positions, attention, feedforward, vectors)
    firsts = (word_first, positions_first, attention_first, feedforward_first, vectors_first)
    seconds = (word_second, positions_second, attention_second, feedforward_second, vectors_second)
    anchors = (word_anchor, positions_anchor, attention_anchor, feedforward_anchor, vectors_anchor)
    outers = (word_outer, positions_outer, attention_outer, feedforward_outer, vectors_outer)
    first_new, second_new, inner_new = ([], [], [])
    for kind in range(5):
        fresh_first, fresh_second, stepped = adam(
            weights[kind], grads[kind] * factor, firsts[kind], seconds[kind]
        )
        first_new.append(fresh_first)
        second_new.append(fresh_second)
        inner_new.append(stepped)
    differences = tuple((anchors[kind] - inner_new[kind][0] for kind in range(5)))
    summed = lax.psum(
        (differences[0], differences[1], differences[2], differences[3], differences[4]), "grp"
    )
    groups = lax.axis_size("grp")
    averages, outer_next, weight_next = ([], [], [])
    for kind in range(5):
        average = summed[kind] / groups
        momentum = OUTER_MU * outers[kind] + average
        outer_weight = anchors[kind] - OUTER_RATE * (average + OUTER_MU * momentum)
        averages.append(average)
        outer_next.append(momentum)
        weight_next.append(outer_weight[None])
    return (
        loss_total.reshape(1),
        count.reshape(1),
        norm.reshape(1),
        first_new[0],
        first_new[1],
        first_new[2],
        first_new[3],
        first_new[4],
        second_new[0],
        second_new[1],
        second_new[2],
        second_new[3],
        second_new[4],
        averages[0],
        averages[1],
        averages[2],
        averages[3],
        averages[4],
        outer_next[0],
        outer_next[1],
        outer_next[2],
        outer_next[3],
        outer_next[4],
        weight_next[0],
        weight_next[1],
        weight_next[2],
        weight_next[3],
        weight_next[4],
    )


def solution(mesh):
    placed = (
        P(("grp", "dp"), None),
        P(("grp", "dp"), None),
        P(("grp", "dp")),
        P(("grp", "dp")),
        P(("grp", "dp")),
        P(("grp", "dp")),
        P(("grp", "dp")),
        P("grp", "dp", None),
        P("grp", None, None, None),
        P("grp", None, None, None),
        P("grp", None, None, None, None),
        P("grp", None, None, None),
        P("grp", "dp", None),
        P("grp", None, None, None),
        P("grp", None, None, None),
        P("grp", None, None, None, None),
        P("grp", None, None, None),
        P("grp", "dp", None),
        P("grp", None, None, None),
        P("grp", None, None, None),
        P("grp", None, None, None, None),
        P("grp", None, None, None),
        P("dp", None),
        P(),
        P(),
        P(),
        P(),
        P("dp", None),
        P(),
        P(),
        P(),
        P(),
    )
    return jax.shard_map(
        body,
        mesh=mesh,
        in_specs=placed,
        out_specs=(
            P("grp"),
            P("grp"),
            P("grp"),
            P("grp", "dp", None),
            P("grp", None, None, None),
            P("grp", None, None, None),
            P("grp", None, None, None, None),
            P("grp", None, None, None),
            P("grp", "dp", None),
            P("grp", None, None, None),
            P("grp", None, None, None),
            P("grp", None, None, None, None),
            P("grp", None, None, None),
            P("dp", None),
            P(),
            P(),
            P(),
            P(),
            P("dp", None),
            P(),
            P(),
            P(),
            P(),
            P("grp", "dp", None),
            P("grp", None, None, None),
            P("grp", None, None, None),
            P("grp", None, None, None, None),
            P("grp", None, None, None),
        ),
        check_vma=False,
    )
```

profile of v0, /device:TPU:0, one launch (start us, length us, event | category | flops | bytes accessed | tf_op | source)
XLA Modules:
  0.0 1194.4 jit_solution(8912217660537799923)
XLA Ops:
  14.5 16.8 %all-reduce.6 = (s32[512]{0:T(512)}, s32[256]{0:T(256)S(1)}, s32[256]{0:T(256)}) all-reduce(s32[512]{0:T(512)S(1)} %dynamic-update-slice.12, s32[256]{0:T(256)S(1)} %dynamic-update-slice.13, s32[256]{0:T(256)S(1)} %dynamic-update-slice.14), channel_id=1, replica_groups=mesh['grp'=2,'dp'=16] {'dp'}, use_global_device_ids=true, to_apply=%add.3 | all-reduce | flops 1024 | bytes 8192
  49.5 72.9 %all-gather.5.cloned.1.call-done = bf16[1,30720,128]{2,1,0:T(8,128)(2,1)} async-done(((bf16[1,1920,128]{2,1,0:T(8,128)(2,1)}), bf16[1,30720,128]{2,1,0:T(8,128)(2,1)}) %all-gather.5.cloned.1.call-update) | async-done | bytes 7864336 | tf_op jit(solution)/shard_map/all_gather | solution.py:269
  122.4 7.1 gather_fusion
  129.5 26.1 %gather_fusion.1 = bf16[8192,128]{1,0:T(8,128)(2,1)S(1)} fusion(bf16[30720,128]{1,0:T(8,128)(2,1)} %bitcast.429, s32[8192]{0:T(1024)S(1)} %broadcast_clamp_fusion), kind=kCustom, calls=%fused_computation.1 | custom fusion | bytes 4227072 | tf_op jit(solution)/shard_map/jit(_take)/gather | solution.py:71
  157.2 6.8 fusion.31
  164.1 7.1 multiply_reduce_fusion.7
  173.5 4.0 reshape.681
  177.5 4.1 fusion.182
  192.2 40.5 %all-gather.2 = bf16[256,1,128]{2,0,1:T(8,128)(2,1)} all-gather(bf16[16,1,128]{2,0,1:T(8,128)(2,1)S(1)} %copy.204), channel_id=4, replica_groups=mesh['grp'=2,'dp'=16] {'dp'}, dimensions={0}, use_global_device_ids=true | all-gather | bytes 69632 | tf_op jit(solution)/shard_map/all_gather | solution.py:281
  232.7 6.4 fusion.33
  240.5 4.9 add_convert_fusion
  245.4 8.6 copy.147
  254.0 9.7 fusion.186
  263.8 10.0 fusion.7
  273.8 10.9 fusion.53
  284.6 4.5 copy.185
  289.2 8.1 fusion.187
  297.3 7.0 multiply_reduce_fusion.6
  307.5 9.7 multiply_convert_fusion.1
  317.2 7.1 fusion.188
  324.4 7.0 multiply_reduce_fusion.5
  334.1 36.5 %all-gather.1 = bf16[512,1,128]{2,0,1:T(8,128)(2,1)S(1)} all-gather(bf16[32,1,128]{2,0,1:T(8,128)(2,1)S(1)} %fusion.141), channel_id=3, replica_groups=mesh['grp'=2,'dp'=16] {'dp'}, dimensions={0}, use_global_device_ids=true | all-gather | bytes 139264 | tf_op jit(solution)/shard_map/all_gather | solution.py:282
  378.3 117.4 %reduce-scatter.3.cloned.1.call-done = f32[48,128]{1,0:T(8,128)} async-done(((f32[768,128]{1,0:T(8,128)}), f32[48,128]{1,0:T(8,128)}) %reduce-scatter.3.cloned.1.call-update) | async-done | bytes 24592 | tf_op jit(solution)/shard_map/reduce_scatter | solution.py:315
  502.8 3.9 convert_reduce_fusion.5
  529.5 9.1 pad_reduce_fusion
  538.7 5.1 fusion.96
  543.9 5.5 convert_reduce_fusion.2
  549.4 5.8 fusion.63
  555.2 16.9 %convert_reduce_fusion = (f32[512]{0:T(512)}, bf16[32,256,512]{2,1,0:T(8,128)(2,1)S(1)}) fusion(f32[32,256,512]{2,1,0:T(8,128)} %get-tuple-element.210, f32[512]{0:T(512)S(1)} %bitcast.477, bf16[1,2,2,128,512]{4,3,2,1,0:T(8,128)(2,1)S(1)} %copy-done.67, bf16[32,256,128]{2,0,1:T(8,128)(2,1)S(1)} %get-tuple-element.160), kind=kOutput, calls=%fused_computation.12 | convolution fusion | flops 1170210304 | bytes 27398144 | tf_op jit(solution)/shard_map/bld,df->blf/dot_general | solution.py:118
  572.1 5.8 fusion.60
  577.9 8.8 multiply_reduce_fusion.1
  586.8 5.2 fusion.181
  605.0 10.0 fusion.35
  615.0 11.0 multiply_reduce_fusion
  626.0 11.8 multiply_convert_fusion
  637.8 4.0 multiply_bitcast_fusion
  649.5 9.0 copy.194
  658.6 5.5 convolution_bitcast_fusion.4
  665.8 10.0 fusion.172
  680.9 9.7 multiply_reduce_fusion.2
  690.7 8.4 fusion.179
  702.1 6.6 copy.173
  708.7 57.9 %scatter_custom_fusion = f32[30720,128]{1,0:T(8,128)} fusion(s32[9216]{0:T(1024)S(1)} %pad_add_fusion, f32[]{:T(128)} %constant.310.clone.1, f32[8192,128]{1,0:T(8,128)} %bitcast.433, f32[]{:T(128)} %constant.314.clone.1, f32[1024,128]{1,0:T(8,128)S(1)} %bitcast.443), kind=kCustom, calls=%fused_computation.31 | custom fusion | flops 2359296 | bytes 20447240 | tf_op jit(solution)/shard_map/scatter-add | solution.py:332
  769.9 53.8 %all-reduce.13.cloned.1.call-done = (f32[2,256,128]{2,1,0:T(8,128)}, f32[2,128,512]{2,1,0:T(8,128)}, f32[2,2,128,512]{3,2,1,0:T(8,128)}) async-done(((f32[2,256,128]{2,1,0:T(8,128)}, f32[2,128,512]{2,1,0:T(8,128)}, f32[2,2,128,512]{3,2,1,0:T(8,128)}), (f32[2,256,128]{2,1,0:T(8,128)}, f32[2,128,512]{2,1,0:T(8,128)}, f32[2,2,128,512]{3,2,1,0:T(8,128)})) %all-reduce.13.cloned.1.call-update) | async-done | bytes 1835024 | tf_op jit(solution)/shard_map/psum | solution.py:335
  831.4 235.4 %reduce-scatter.5.cloned.1.call-done = f32[1920,128]{1,0:T(8,128)} async-done(((f32[30720,128]{1,0:T(8,128)}), f32[1920,128]{1,0:T(8,128)}) %reduce-scatter.5.cloned.1.call-update) | async-done | bytes 983056 | tf_op jit(solution)/shard_map/reduce_scatter | solution.py:333
  1068.9 76.0 %all-reduce.7 = (f32[1]{0:T(128)}, f32[]{:T(128)}, f32[2,14,128]{2,0,1:T(2,128)S(1)}) all-reduce(f32[1]{0:T(128)} %bitcast.57, f32[]{:T(128)} %multiply_reduce_fusion.10, f32[2,14,128]{2,0,1:T(2,128)S(1)} %pad_maximum_fusion.3), channel_id=1, replica_groups=mesh['grp'=2,'dp'=16] {'dp'}, use_global_device_ids=true, to_apply=%region_25.26 | all-reduce | flops 3586 | bytes 28688 | tf_op jit(solution)/shard_map/psum | solution.py:321
  1158.9 3.3 psum.87
  1162.8 14.1 %all-reduce.15.cloned.1.call-done = (f32[1920,128]{1,0:T(8,128)}, f32[2,256,128]{2,1,0:T(8,128)}, f32[2,128,512]{2,1,0:T(8,128)}, f32[2,2,128,512]{3,2,1,0:T(8,128)}) async-done(((f32[1920,128]{1,0:T(8,128)}, f32[2,256,128]{2,1,0:T(8,128)}, f32[2,128,512]{2,1,0:T(8,128)}, f32[2,2,128,512]{3,2,1,0:T(8,128)}), (f32[1920,128]{1,0:T(8,128)}, f32[2,256,128]{2,1,0:T(8,128)}, f32[2,128,512]{2,1,0:T(8,128)}, ...) | async-done | bytes 2818064 | tf_op jit(solution)/shard_map/psum | solution.py:357
  (566 shorter events, 142.5 us)
Async XLA Ops:
  7.2 41.6 %copy-start.46 = (f32[1,2,128,512]{3,2,1,0:T(8,128)S(1)}, f32[1,2,128,512]{3,2,1,0:T(8,128)}, u32[]{:S(2)}) copy-start(f32[1,2,128,512]{3,2,1,0:T(8,128)} %param.51) | copy-start | bytes 1572868
  7.2 115.2 %all-gather.5.cloned.1.call-start = ((), (), s32[]{:S(2)}) async-start(), calls=%async_computation.4 | async-start | bytes 8355840 | tf_op jit(solution)/shard_map/all_gather | solution.py:269
  9.4 486.3 %reduce-scatter.3.cloned.1.call-start = ((), (), s32[]{:S(2)}) async-start(), calls=%async_computation.2 | async-start | bytes 417792 | tf_op jit(solution)/shard_map/reduce_scatter | solution.py:315
  34.3 129.8 %copy-start.43 = (pred[32,256]{0,1:T(8,128)(4,1)}, pred[32,256]{0,1:T(8,128)(4,1)S(1)}, u32[]{:S(2)}) copy-start(pred[32,256]{0,1:T(8,128)(4,1)S(1)} %copy.144) | copy-start | bytes 24580
  37.7 117.9 %copy-start.152 = (s32[32]{0:T(128)}, s32[32]{0:T(128)S(1)}, u32[]{:S(2)}) copy-start(s32[32]{0:T(128)S(1)} %and_select_fusion) | copy-start | bytes 388
  39.2 132.7 %copy-start.139 = (f32[128]{0:T(128)}, f32[128]{0:T(128)S(1)}, u32[]{:S(2)}) copy-start(f32[128]{0:T(128)S(1)} %get-tuple-element.194) | copy-start | bytes 1540
  39.2 132.7 %copy-start.184 = (f32[128]{0:T(128)}, f32[128]{0:T(128)S(1)}, u32[]{:S(2)}) copy-start(f32[128]{0:T(128)S(1)} %get-tuple-element.193) | copy-start | bytes 1540
  47.1 124.8 %copy-start.116 = (pred[16,64]{1,0:T(8,128)(4,1)}, pred[16,64]{1,0:T(8,128)(4,1)S(1)}, u32[]{:S(2)}) copy-start(pred[16,64]{1,0:T(8,128)(4,1)S(1)} %compare_and_fusion.1) | copy-start | bytes 3076
  47.8 124.1 %copy-start.68 = (f32[64,128]{1,0:T(8,128)}, f32[64,128]{1,0:T(8,128)S(1)}, u32[]{:S(2)}) copy-start(f32[64,128]{1,0:T(8,128)S(1)} %slice_bitcast_fusion.30) | copy-start | bytes 98308
  48.8 240.4 %copy-start.16 = (f32[256,128]{1,0:T(8,128)}, f32[256,128]{1,0:T(8,128)S(1)}, u32[]{:S(2)}) copy-start(f32[256,128]{1,0:T(8,128)S(1)} %slice_bitcast_fusion.13) | copy-start | bytes 393220
  49.5 122.4 %copy-start.92 = (bf16[128,512]{1,0:T(8,128)(2,1)}, bf16[128,512]{1,0:T(8,128)(2,1)S(1)}, u32[]{:S(2)}) copy-start(bf16[128,512]{1,0:T(8,128)(2,1)S(1)} %get-tuple-element.174) | copy-start | bytes 393220
  155.7 133.5 %copy-start.2 = (bf16[8192,128]{1,0:T(8,128)(2,1)}, bf16[8192,128]{1,0:T(8,128)(2,1)S(1)}, u32[]{:S(2)}) copy-start(bf16[8192,128]{1,0:T(8,128)(2,1)S(1)} %gather_fusion.1) | copy-start | bytes 6291460
  188.5 44.2 %copy-start.28 = (f32[32,256]{0,1:T(8,128)S(1)}, f32[32,256]{0,1:T(8,128)}, u32[]{:S(2)}) copy-start(f32[32,256]{0,1:T(8,128)} %copy-done.27) | copy-start | bytes 98308
  188.5 44.2 %copy-start.30 = (f32[32,256]{0,1:T(8,128)S(1)}, f32[32,256]{0,1:T(8,128)}, u32[]{:S(2)}) copy-start(f32[32,256]{0,1:T(8,128)} %fusion.104) | copy-start | bytes 98308
  188.5 44.1 %copy-start.44 = (pred[32,256]{0,1:T(8,128)(4,1)S(1)}, pred[32,256]{0,1:T(8,128)(4,1)}, u32[]{:S(2)}) copy-start(pred[32,256]{0,1:T(8,128)(4,1)} %copy-done.43) | copy-start | bytes 24580
  188.5 44.1 %copy-start.131 = (f32[128]{0:T(128)S(1)}, f32[128]{0:T(128)}, u32[]{:S(2)}) copy-start(f32[128]{0:T(128)} %get-tuple-element.185) | copy-start | bytes 1540
  188.5 44.1 %copy-start.165 = (f32[128]{0:T(128)S(1)}, f32[128]{0:T(128)}, u32[]{:S(2)}) copy-start(f32[128]{0:T(128)} %get-tuple-element.184) | copy-start | bytes 1540
  190.8 48.3 %copy-start.21 = (bf16[16,64,512]{2,1,0:T(8,128)(2,1)}, bf16[16,64,512]{2,1,0:T(8,128)(2,1)S(1)}, u32[]{:S(2)}) copy-start(bf16[16,64,512]{2,1,0:T(8,128)(2,1)S(1)} %get-tuple-element.217) | copy-start | bytes 3145732
  190.8 49.7 %copy-start.74 = (bf16[128,512]{1,0:T(8,128)(2,1)S(1)}, bf16[128,512]{1,0:T(8,128)(2,1)}, u32[]{:S(2)}) copy-start(bf16[128,512]{1,0:T(8,128)(2,1)} %get-tuple-element.175) | copy-start | bytes 393220
  190.8 49.7 %copy-start.136 = (f32[384]{0:T(512)S(1)}, f32[384]{0:T(512)}, u32[]{:S(2)}) copy-start(f32[384]{0:T(512)} %get-tuple-element.204) | copy-start | bytes 4612
  191.8 47.4 %copy-start.106 = (f32[16,64]{1,0:T(8,128)}, f32[16,64]{1,0:T(8,128)S(1)}, u32[]{:S(2)}) copy-start(f32[16,64]{1,0:T(8,128)S(1)} %multiply_reduce_fusion.16) | copy-start | bytes 12292
  191.8 47.4 %copy-start.89 = (f32[16,64]{1,0:T(8,128)}, f32[16,64]{1,0:T(8,128)S(1)}, u32[]{:S(2)}) copy-start(f32[16,64]{1,0:T(8,128)S(1)} %fusion.159) | copy-start | bytes 12292
  192.2 47.0 %copy-start.119 = (bf16[16,1,128]{2,0,1:T(8,128)(2,1)}, bf16[16,1,128]{2,0,1:T(8,128)(2,1)S(1)}, u32[]{:S(2)}) copy-start(bf16[16,1,128]{2,0,1:T(8,128)(2,1)S(1)} %copy.204) | copy-start | bytes 12292
  331.4 39.2 %copy-start.113 = (bf16[256,1,128]{2,0,1:T(8,128)(2,1)S(1)}, bf16[256,1,128]{2,0,1:T(8,128)(2,1)}, u32[]{:S(2)}) copy-start(bf16[256,1,128]{2,0,1:T(8,128)(2,1)} %all-gather.2) | copy-start | bytes 196612
  331.4 39.2 %copy-start.153 = (s32[32]{0:T(128)S(1)}, s32[32]{0:T(128)}, u32[]{:S(2)}) copy-start(s32[32]{0:T(128)} %copy-done.152) | copy-start | bytes 388
  331.4 39.2 %copy-start.154 = (s32[256]{0:T(256)S(1)}, s32[256]{0:T(256)}, u32[]{:S(2)}) copy-start(s32[256]{0:T(256)} %get-tuple-element.110) | copy-start | bytes 3076
  331.5 39.2 %copy-start.170 = (s32[32]{0:T(128)S(1)}, s32[32]{0:T(128)}, u32[]{:S(2)}) copy-start(s32[32]{0:T(128)} %param.47) | copy-start | bytes 388
  331.5 39.2 %copy-start.172 = (pred[256]{0:T(512)(128)(4,1)S(1)}, pred[256]{0:T(512)(128)(4,1)}, u32[]{:S(2)}) copy-start(pred[256]{0:T(512)(128)(4,1)} %broadcast_compare_fusion) | copy-start | bytes 772
  331.5 40.8 %copy-start.177 = (f32[32]{0:T(128)S(1)}, f32[32]{0:T(128)}, u32[]{:S(2)}) copy-start(f32[32]{0:T(128)} %get-tuple-element.169) | copy-start | bytes 388
  331.5 41.1 %copy-start.120 = (bf16[16,1,128]{2,0,1:T(8,128)(2,1)S(1)}, bf16[16,1,128]{2,0,1:T(8,128)(2,1)}, u32[]{:S(2)}) copy-start(bf16[16,1,128]{2,0,1:T(8,128)(2,1)} %copy-done.119) | copy-start | bytes 12292
  331.5 41.1 %copy-start.138 = (s32[512]{0:T(512)S(1)}, s32[512]{0:T(512)}, u32[]{:S(2)}) copy-start(s32[512]{0:T(512)} %get-tuple-element.108) | copy-start | bytes 6148
  331.5 41.1 %copy-start.156 = (s32[16]{0:T(128)S(1)}, s32[16]{0:T(128)}, u32[]{:S(2)}) copy-start(s32[16]{0:T(128)} %param.46) | copy-start | bytes 196
  331.5 41.1 %copy-start.157 = (s32[16]{0:T(128)S(1)}, s32[16]{0:T(128)}, u32[]{:S(2)}) copy-start(s32[16]{0:T(128)} %add_multiply_fusion) | copy-start | bytes 196
  331.5 41.6 %copy-start.181 = (s32[16]{0:T(128)S(1)}, s32[16]{0:T(128)}, u32[]{:S(2)}) copy-start(s32[16]{0:T(128)} %param.48) | copy-start | bytes 196
  331.5 46.1 %copy-start.73 = (f32[32,2,256]{2,1,0:T(2,128)S(1)}, f32[32,2,256]{2,1,0:T(2,128)}, u32[]{:S(2)}) copy-start(f32[32,2,256]{2,1,0:T(2,128)} %copy-done.72) | copy-start | bytes 196612
  331.6 46.1 %copy-start.84 = (f32[32,2,256]{2,1,0:T(2,128)S(1)}, f32[32,2,256]{2,1,0:T(2,128)}, u32[]{:S(2)}) copy-start(f32[32,2,256]{2,1,0:T(2,128)} %copy-done.83) | copy-start | bytes 196612
  331.6 165.2 %copy-start.90 = (f32[16,64]{1,0:T(8,128)S(1)}, f32[16,64]{1,0:T(8,128)}, u32[]{:S(2)}) copy-start(f32[16,64]{1,0:T(8,128)} %copy-done.89) | copy-start | bytes 12292
  331.6 167.0 %copy-start.107 = (f32[16,64]{1,0:T(8,128)S(1)}, f32[16,64]{1,0:T(8,128)}, u32[]{:S(2)}) copy-start(f32[16,64]{1,0:T(8,128)} %copy-done.106) | copy-start | bytes 12292
  334.1 167.6 %copy-start.22 = (bf16[16,64,512]{2,1,0:T(8,128)(2,1)S(1)}, bf16[16,64,512]{2,1,0:T(8,128)(2,1)}, u32[]{:S(2)}) copy-start(bf16[16,64,512]{2,1,0:T(8,128)(2,1)} %copy-done.21) | copy-start | bytes 3145732
  370.9 135.7 %copy-start.99 = (f32[32,256]{1,0:T(8,128)}, f32[32,256]{1,0:T(8,128)S(1)}, u32[]{:S(2)}) copy-start(f32[32,256]{1,0:T(8,128)S(1)} %get-tuple-element.224) | copy-start | bytes 98308
  376.3 447.4 %all-reduce.13.cloned.1.call-start = ((), (), s32[]{:S(2)}) async-start(), calls=%async_computation.5 | async-start | bytes 3670016 | tf_op jit(solution)/shard_map/psum | solution.py:335
  525.6 150.3 %copy-start.34 = (f32[16,64,128]{2,1,0:T(8,128)}, f32[16,64,128]{2,1,0:T(8,128)S(1)}, u32[]{:S(2)}) copy-start(f32[16,64,128]{2,1,0:T(8,128)S(1)} %get-tuple-element.232) | copy-start | bytes 1572868
  702.0 364.9 %reduce-scatter.5.cloned.1.call-start = ((), (), s32[]{:S(2)}) async-start(), calls=%async_computation.3 | async-start | bytes 16711680 | tf_op jit(solution)/shard_map/reduce_scatter | solution.py:333
  766.9 380.1 %copy-start.56 = (f32[2,256,128]{2,1,0:T(8,128)S(1)}, f32[2,256,128]{2,1,0:T(8,128)}, u32[]{:S(2)}) copy-start(f32[2,256,128]{2,1,0:T(8,128)} %param.65) | copy-start | bytes 786436
  766.9 410.0 %all-reduce.15.cloned.1.call-start = ((), (), s32[]{:S(2)}) async-start(), calls=%async_computation.6 | async-start | bytes 5636096 | tf_op jit(solution)/shard_map/psum | solution.py:357
  827.1 325.4 %copy-start.18 = (f32[1,2,2,128,512]{4,3,2,1,0:T(8,128)S(1)}, f32[1,2,2,128,512]{4,3,2,1,0:T(8,128)}, u32[]{:S(2)}) copy-start(f32[1,2,2,128,512]{4,3,2,1,0:T(8,128)} %param.52) | copy-start | bytes 3145732
  827.1 325.4 %copy-start.19 = (f32[2,2,128,512]{3,2,1,0:T(8,128)S(1)}, f32[2,2,128,512]{3,2,1,0:T(8,128)}, u32[]{:S(2)}) copy-start(f32[2,2,128,512]{3,2,1,0:T(8,128)} %get-tuple-element.116) | copy-start | bytes 3145732
  827.1 325.4 %copy-start.20 = (f32[2,2,128,512]{3,2,1,0:T(8,128)S(1)}, f32[2,2,128,512]{3,2,1,0:T(8,128)}, u32[]{:S(2)}) copy-start(f32[2,2,128,512]{3,2,1,0:T(8,128)} %param.67) | copy-start | bytes 3145732
  (155 other events, 913.0 us)
Sparse Core Ops, SparseCore 0:
  11.4 110.9 all-gather.4
  376.4 119.2 reduce-scatter.2
  702.1 121.5 all-reduce.12
  829.2 237.6 reduce-scatter.4
  1158.3 18.5 all-reduce.14
where the time goes:
time: 1200 us; the launch traced here: 1190 us
  waiting for transfers between devices  494 us (41%)
  other arithmetic  232 us (19%)
  blocking collectives  173 us (14%)
  matrix products  166 us (14%)
  local copies, waits for them, and re-layouts  104 us (9%)
  between operations  25.9 us (2%)
    reduce_scatter x1, waiting for transfers between devices, body(): lax.psum_scatter(table_full, 'dp', scatter_dimension=0, tiled=True)  235 us
    reduce_scatter x1, waiting for transfers between devices, body(): lax.psum_scatter(joined.reshape(many * rows_each, -1), 'dp', scatter_dime...  117 us
    psum x1, blocking collectives, body(): loss_total = lax.psum(loss_local, 'dp')  76 us
    all_gather x1, waiting for transfers between devices, body(): wide = lax.all_gather(low16(word_table[0]), 'dp', axis=0, tiled=True)  72.9 us
    scatter-add x1, other arithmetic, body(): jax.ops.segment_sum(token_grads, token_ids, num_segments=wide.shape[0])  57.9 us
    psum x1, waiting for transfers between devices, body(): lax.psum((stacked[0], stacked[1], stacked[2], stacked[3]), 'dp')  53.8 us
    all_gather x1, blocking collectives, body(): lax.all_gather(own_q, 'dp', axis=0, tiled=True)  40.5 us
    all_gather x1, blocking collectives, body(): lax.all_gather(own_p, 'dp', axis=0, tiled=True)  36.5 us
  transfers between devices with their start and end apart: 5, of which 5 were waited for; matrix products, arithmetic and copies ran while one was open for 8% of the time, Pallas kernels for 0%

commit v1 on v0

v1 whole, which is shorter than its diff:
```python
import jax
import jax.numpy as jnp
from jax import lax
from jax.sharding import PartitionSpec as P

HEAD = 64
STEP = 5


NORM_EPS = 1e-05
MASKED = -1000000000.0
BETA_ONE = 0.9
BETA_TWO = 0.999
INNER_RATE = 0.05
WEIGHT_DECAY = 0.01
ADAM_EPS = 1e-08
CLIP_LIMIT = 0.01
OUTER_RATE = 0.7
OUTER_MU = 0.9
CONTRACT_ROWS = (((0,), (0,)), ((), ()))
CONTRACT_LAST = (((1,), (1,)), ((), ()))


def layer_norm(values, gain, shift):
    center = values - jnp.mean(values, -1, keepdims=True)
    spread = jnp.mean(center * center, -1, keepdims=True)
    return center * lax.rsqrt(spread + NORM_EPS) * gain + shift


def gelu_tanh(values):
    return jax.nn.gelu(values, approximate=True)


def low16(values):
    return values.astype(jnp.bfloat16)


def dot(left, right):
    return jnp.dot(left, right, preferred_element_type=jnp.float32)


def dot_rows(left, right):
    return lax.dot_general(left, right, CONTRACT_ROWS, preferred_element_type=jnp.float32)


def dot_last(left, right):
    return lax.dot_general(left, right, CONTRACT_LAST, preferred_element_type=jnp.float32)


def token_forward(rows, place, attn_w, vec, lengths):
    sequences, seq, width = rows.shape
    heads = width // HEAD
    x_embed = rows.astype(jnp.float32) + place[:seq]
    a_low = low16(layer_norm(x_embed, vec[0], vec[1]))
    w_kv = low16(attn_w[:, width : 3 * width])
    bias = jnp.concatenate([jnp.zeros_like(vec[3]), vec[3]])
    kv = low16(
        jnp.einsum("bld,de->ble", a_low, w_kv, preferred_element_type=jnp.float32) + bias
    ).reshape(sequences, seq, 2, heads, HEAD)
    query = low16(dot(a_low[:, 0], low16(attn_w[:, :width])) + vec[2]).reshape(
        sequences, heads, HEAD
    )
    keys_all, values_all = kv[:, :, 0], kv[:, :, 1]
    scores = jnp.einsum(
        "bhe,bkhe->bhk", query, keys_all, preferred_element_type=jnp.float32
    ) * HEAD ** (-0.5)
    keep = jnp.arange(seq)[None, None, :] < lengths[:, None, None]
    scores = jnp.where(keep, scores, MASKED)
    top = jnp.max(scores, -1, keepdims=True)
    expo = jnp.exp(scores - top)
    probs = expo / jnp.sum(expo, -1, keepdims=True)
    mixed = jnp.einsum(
        "bhk,bkhe->bhe", low16(probs), values_all, preferred_element_type=jnp.float32
    )
    mixed = low16(mixed.reshape(sequences, width))
    return mixed, (x_embed, a_low, query, keys_all, values_all, probs)


def token_backward(kept, attn_w, vec, d_mixed, d_x_attn):
    x_embed, a_low, query, keys_all, values_all, probs = kept
    sequences, seq, width = x_embed.shape
    heads = width // HEAD
    dm = d_mixed.reshape(sequences, heads, HEAD)
    d_probs = jnp.einsum("bhe,bkhe->bhk", dm, values_all, preferred_element_type=jnp.float32)
    d_values = low16(probs).astype(jnp.float32).transpose(0, 2, 1)[..., None] * dm.astype(
        jnp.float32
    )[:, None]
    d_scores = low16(probs * (d_probs - jnp.sum(probs * d_probs, -1, keepdims=True)))
    d_query = jnp.einsum(
        "bhk,bkhe->bhe", d_scores, keys_all, preferred_element_type=jnp.float32
    ) * HEAD ** (-0.5)
    d_keys = (
        d_scores.astype(jnp.float32).transpose(0, 2, 1)[..., None]
        * query.astype(jnp.float32)[:, None]
        * HEAD ** (-0.5)
    )
    d_query = low16(d_query.reshape(sequences, width))
    d_kv = low16(
        jnp.concatenate(
            [
                d_keys.reshape(sequences, seq, width),
                d_values.reshape(sequences, seq, width),
            ],
            -1,
        )
    )
    d_query_bias = jnp.sum(d_query.astype(jnp.float32), 0)
    d_value_bias = jnp.sum(d_kv[..., width:], (0, 1), dtype=jnp.float32)
    d_w_kv = jnp.einsum("bld,ble->de", a_low, d_kv, preferred_element_type=jnp.float32)
    d_w_q = dot_rows(a_low[:, 0], d_query)
    w_low = low16(attn_w)
    d_h = jnp.einsum(
        "ble,de->bld", d_kv, w_low[:, width : 3 * width], preferred_element_type=jnp.float32
    )
    first = d_x_attn + dot_last(d_query, w_low[:, :width])
    d_h = d_h.at[:, 0].add(first)
    unused, embed_back = jax.vjp(layer_norm, x_embed, vec[0], vec[1])
    d_x_embed, d_gain, d_shift = embed_back(d_h)
    return d_x_embed, jnp.concatenate([d_w_q, d_w_kv], 1), (d_gain, d_shift, d_query_bias, d_value_bias)


def class_forward(rows, mixed, place, attn_w, ffn_w, vec):
    width = rows.shape[1]
    h_embed = layer_norm(rows.astype(jnp.float32) + place[:1], vec[0], vec[1])
    x_attn = h_embed + (dot(mixed, low16(attn_w[:, 3 * width :])) + vec[4])
    h_attn = layer_norm(x_attn, vec[5], vec[6])
    h_low = low16(h_attn)
    pre = dot(h_low, low16(ffn_w[0])) + vec[10:].reshape(-1)
    act = low16(gelu_tanh(pre))
    x_ffn = h_attn + (dot_last(act, low16(ffn_w[1])) + vec[7])
    h_out = layer_norm(x_ffn, vec[8], vec[9])
    return low16(h_out), (x_attn, h_low, pre, act, x_ffn)


def class_backward(kept, mixed, attn_w, ffn_w, vec, d_cls):
    x_attn, h_low, pre, act, x_ffn = kept
    width = x_attn.shape[1]
    unused, out_back = jax.vjp(layer_norm, x_ffn, vec[8], vec[9])
    d_x_ffn, d_gain_two, d_shift_two = out_back(d_cls)
    d_branch = low16(d_x_ffn)
    d_down_bias = jnp.sum(d_branch, 0, dtype=jnp.float32)
    d_down = dot_rows(d_branch, act)
    d_act = dot(d_branch, low16(ffn_w[1]))
    unused, gelu_back = jax.vjp(gelu_tanh, pre)
    d_pre = low16(gelu_back(d_act)[0])
    d_up_bias = jnp.sum(d_pre, 0, dtype=jnp.float32)
    d_up = dot_rows(h_low, d_pre)
    d_h_attn = d_x_ffn + dot_last(d_pre, low16(ffn_w[0]))
    unused, attn_back = jax.vjp(layer_norm, x_attn, vec[5], vec[6])
    d_x_attn, d_gain_one, d_shift_one = attn_back(d_h_attn)
    d_proj = low16(d_x_attn)
    d_out_bias = jnp.sum(d_proj, 0, dtype=jnp.float32)
    d_w_out = dot_rows(mixed, d_proj)
    d_mixed = low16(dot_last(d_proj, low16(attn_w[:, 3 * width :])))
    rows = (d_out_bias, d_gain_one, d_shift_one, d_down_bias, d_gain_two, d_shift_two)
    return d_mixed, d_x_attn, d_w_out, jnp.stack([d_up, d_down]), rows, d_up_bias


def softmax_terms(scores, drop, target, weight, count, axis):
    masked = jnp.where(drop, MASKED, scores)
    top = jnp.max(masked, axis, keepdims=True)
    expo = jnp.exp(masked - top)
    total = jnp.sum(expo, axis, keepdims=True)
    lse = top + jnp.log(total)
    picked = jnp.sum(jnp.where(target, scores, 0.0), axis, keepdims=True)
    loss = jnp.sum(weight * (lse - picked))
    grad = low16((weight / count) * (expo / total - target.astype(jnp.float32)))
    return grad, loss


def score_stage(every_q, every_p, keys_q, keys_p, valid_q):
    count = jnp.maximum(jnp.sum(valid_q).astype(jnp.float32), 1.0)
    scale = every_q.shape[1] ** (-0.5)
    index_q = jnp.arange(every_q.shape[0])[:, None]
    index_p = jnp.arange(every_p.shape[0])[None, :]
    scores = dot_last(every_q, every_p) * scale
    same = keys_q[:, None] == keys_p[None, :]
    target_qp = index_p == 2 * index_q
    valid = valid_q.astype(jnp.float32)[:, None]
    grad_qp, loss_qp = softmax_terms(scores, same & ~target_qp, target_qp, valid, count, 1)
    target_pq = index_p // 2 == index_q
    drop_pq = (same | (valid_q[:, None] == 0)) & ~target_pq
    owner_valid = jnp.repeat(valid_q, 2)
    weight_p = jnp.where(index_p[0] % 2 == 0, owner_valid, 0).astype(jnp.float32)[None, :]
    grad_pq, loss_pq = softmax_terms(scores, drop_pq, target_pq, weight_p, count, 0)
    d_q = (dot(grad_qp, every_p) + dot(grad_pq, every_p)) * scale
    d_p = (dot_rows(grad_pq, every_q) + dot_rows(grad_qp, every_q)) * scale
    return d_q, d_p, loss_qp + loss_pq, count


def adam(weight, grad, first, second):
    first_new = BETA_ONE * first + (1.0 - BETA_ONE) * grad
    second_new = BETA_TWO * second + (1.0 - BETA_TWO) * grad * grad
    fix_one = 1.0 - BETA_ONE**STEP
    fix_two = 1.0 - BETA_TWO**STEP
    ratio = first_new / fix_one / (jnp.sqrt(second_new / fix_two) + ADAM_EPS)
    return (first_new, second_new, weight - INNER_RATE * (ratio + WEIGHT_DECAY * weight))


def body(
    question_ids,
    passage_ids,
    question_lengths,
    passage_lengths,
    question_keys,
    passage_keys,
    question_valid,
    word_table,
    positions,
    attention,
    feedforward,
    vectors,
    word_first,
    positions_first,
    attention_first,
    feedforward_first,
    vectors_first,
    word_second,
    positions_second,
    attention_second,
    feedforward_second,
    vectors_second,
    word_anchor,
    positions_anchor,
    attention_anchor,
    feedforward_anchor,
    vectors_anchor,
    word_outer,
    positions_outer,
    attention_outer,
    feedforward_outer,
    vectors_outer,
):
    width = word_table.shape[2]
    wide = lax.all_gather(low16(word_table[0]), "dp", axis=0, tiled=True)
    device = lax.axis_index("dp")
    many = lax.axis_size("dp")
    ids = (question_ids, passage_ids)
    lengths = (question_lengths, passage_lengths)
    counts = (question_ids.shape[0], passage_ids.shape[0])
    flags = jnp.concatenate([question_keys, question_valid, passage_keys])
    flags_all = lax.all_gather(flags, "dp")
    keys_q = flags_all[:, : counts[0]].reshape(-1)
    valid_all = flags_all[:, counts[0] : 2 * counts[0]].reshape(-1)
    keys_p = flags_all[:, 2 * counts[0] :].reshape(-1)
    packs, kepts = ([], [])
    for enc in range(2):
        rows = jnp.take(wide, ids[enc], axis=0)
        mixed, kept = token_forward(
            rows, positions[0, enc], attention[0, enc], vectors[0, enc], lengths[enc]
        )
        packs.append(jnp.concatenate([rows[:, 0], mixed], 1))
        kepts.append(kept)
    every = lax.all_gather(jnp.concatenate(packs), "dp")
    cls, class_kept, mixes = ([], [], [])
    for enc in range(2):
        part = every[:, : counts[0]] if enc == 0 else every[:, counts[0] :]
        part = part.reshape(-1, 2 * width)
        low_cls, kept = class_forward(
            part[:, :width],
            part[:, width:],
            positions[0, enc],
            attention[0, enc],
            feedforward[0, enc],
            vectors[0, enc],
        )
        cls.append(low_cls)
        class_kept.append(kept)
        mixes.append(part[:, width:])
    d_q, d_p, loss_total, count = score_stage(cls[0], cls[1], keys_q, keys_p, valid_all)
    d_cls = (d_q, d_p)
    token_grads, partials, finals = ([], [], [])
    for enc in range(2):
        d_mixed, d_x_attn, d_w_out, d_ffn, rows_mid, d_up_bias = class_backward(
            class_kept[enc], mixes[enc], attention[0, enc], feedforward[0, enc], vectors[0, enc], d_cls[enc]
        )
        begin = device * counts[enc]
        own_mixed = lax.dynamic_slice_in_dim(d_mixed, begin, counts[enc])
        own_x = lax.dynamic_slice_in_dim(d_x_attn, begin, counts[enc])
        d_x_embed, d_w_qkv, rows_first = token_backward(
            kepts[enc], attention[0, enc], vectors[0, enc], own_mixed, own_x
        )
        token_grads.append(d_x_embed)
        place_sum = jnp.sum(d_x_embed, 0)
        d_place = jnp.pad(place_sum, ((0, positions.shape[2] - place_sum.shape[0]), (0, 0)))
        partials.append((d_place, d_w_qkv, jnp.stack(rows_first)))
        finals.append((d_w_out, d_ffn, rows_mid, d_up_bias))
    token_ids = jnp.concatenate([ids[0].reshape(-1), ids[1].reshape(-1)])
    token_all = jnp.concatenate([token_grads[0].reshape(-1, width), token_grads[1].reshape(-1, width)])
    table_full = jax.ops.segment_sum(token_all, token_ids, num_segments=wide.shape[0])
    table_grad = lax.psum_scatter(
        low16(table_full), "dp", scatter_dimension=0, tiled=True
    ).astype(jnp.float32)
    table_sq = jnp.sum(table_grad * table_grad)
    flat = jnp.concatenate(
        [table_sq.reshape(1)] + [v.reshape(-1) for part in partials for v in part]
    )
    flat = lax.psum(flat, "dp")
    table_sq = flat[0]
    spot = 1
    places, attns, vecs = ([], [], [])
    for enc in range(2):
        got = []
        for piece in partials[enc]:
            got.append(flat[spot : spot + piece.size].reshape(piece.shape))
            spot += piece.size
        d_w_out, d_ffn, rows_mid, d_up_bias = finals[enc]
        places.append(got[0])
        attns.append(jnp.concatenate([got[1], d_w_out], 1))
        vecs.append(
            jnp.concatenate([got[2], jnp.stack(rows_mid), d_up_bias.reshape(-1, width)])
        )
    place_grad, attn_grad, vec_grad = (jnp.stack(places), jnp.stack(attns), jnp.stack(vecs))
    ffn_grad = jnp.stack([finals[0][1], finals[1][1]])
    grads = (table_grad[None], place_grad[None], attn_grad[None], ffn_grad[None], vec_grad[None])
    norm = jnp.sqrt(table_sq + sum((jnp.sum(g * g) for g in grads[1:])))
    factor = CLIP_LIMIT / jnp.maximum(norm, CLIP_LIMIT)
    weights = (word_table, positions, attention, feedforward, vectors)
    firsts = (word_first, positions_first, attention_first, feedforward_first, vectors_first)
    seconds = (word_second, positions_second, attention_second, feedforward_second, vectors_second)
    anchors = (word_anchor, positions_anchor, attention_anchor, feedforward_anchor, vectors_anchor)
    outers = (word_outer, positions_outer, attention_outer, feedforward_outer, vectors_outer)
    first_new, second_new, inner_new = ([], [], [])
    for kind in range(5):
        fresh_first, fresh_second, stepped = adam(
            weights[kind], grads[kind] * factor, firsts[kind], seconds[kind]
        )
        first_new.append(fresh_first)
        second_new.append(fresh_second)
        inner_new.append(stepped)
    differences = tuple((anchors[kind] - inner_new[kind][0] for kind in range(5)))
    summed = lax.psum(
        (differences[0], differences[1], differences[2], differences[3], differences[4]), "grp"
    )
    groups = lax.axis_size("grp")
    averages, outer_next, weight_next = ([], [], [])
    for kind in range(5):
        average = summed[kind] / groups
        momentum = OUTER_MU * outers[kind] + average
        outer_weight = anchors[kind] - OUTER_RATE * (average + OUTER_MU * momentum)
        averages.append(average)
        outer_next.append(momentum)
        weight_next.append(outer_weight[None])
    return (
        loss_total.reshape(1),
        count.reshape(1),
        norm.reshape(1),
        first_new[0],
        first_new[1],
        first_new[2],
        first_new[3],
        first_new[4],
        second_new[0],
        second_new[1],
        second_new[2],
        second_new[3],
        second_new[4],
        averages[0],
        averages[1],
        averages[2],
        averages[3],
        averages[4],
        outer_next[0],
        outer_next[1],
        outer_next[2],
        outer_next[3],
        outer_next[4],
        weight_next[0],
        weight_next[1],
        weight_next[2],
        weight_next[3],
        weight_next[4],
    )


def solution(mesh):
    placed = (
        P(("grp", "dp"), None),
        P(("grp", "dp"), None),
        P(("grp", "dp")),
        P(("grp", "dp")),
        P(("grp", "dp")),
        P(("grp", "dp")),
        P(("grp", "dp")),
        P("grp", "dp", None),
        P("grp", None, None, None),
        P("grp", None, None, None),
        P("grp", None, None, None, None),
        P("grp", None, None, None),
        P("grp", "dp", None),
        P("grp", None, None, None),
        P("grp", None, None, None),
        P("grp", None, None, None, None),
        P("grp", None, None, None),
        P("grp", "dp", None),
        P("grp", None, None, None),
        P("grp", None, None, None),
        P("grp", None, None, None, None),
        P("grp", None, None, None),
        P("dp", None),
        P(),
        P(),
        P(),
        P(),
        P("dp", None),
        P(),
        P(),
        P(),
        P(),
    )
    return jax.shard_map(
        body,
        mesh=mesh,
        in_specs=placed,
        out_specs=(
            P("grp"),
            P("grp"),
            P("grp"),
            P("grp", "dp", None),
            P("grp", None, None, None),
            P("grp", None, None, None),
            P("grp", None, None, None, None),
            P("grp", None, None, None),
            P("grp", "dp", None),
            P("grp", None, None, None),
            P("grp", None, None, None),
            P("grp", None, None, None, None),
            P("grp", None, None, None),
            P("dp", None),
            P(),
            P(),
            P(),
            P(),
            P("dp", None),
            P(),
            P(),
            P(),
            P(),
            P("grp", "dp", None),
            P("grp", None, None, None),
            P("grp", None, None, None),
            P("grp", None, None, None, None),
            P("grp", None, None, None),
        ),
        check_vma=False,
    )
```

time: 1200 us -> 782 us (0.65)
  waiting for transfers between devices: 494 us -> 331 us
  blocking collectives: 173 us -> 59.7 us
  matrix products: 166 us -> 54 us
  other arithmetic: 232 us -> 171 us
  local copies, waits for them, and re-layouts: 104 us -> 135 us
    reduce_scatter x2 -> x1, waiting for transfers between devices: 353 us -> 138 us  [body(): lax.psum_scatter(low16(table_full), 'dp', scatter_dimension=0, tiled=True)]
    dot_general x42 -> x43, matrix products: 166 us -> 54 us  [the longest x10 11.6 us: dot(): return jnp.dot(left, right, preferred_element_type=jnp.float32)]
    psum x1 -> x0, blocking collectives: 76 us -> none  [body(): loss_total = lax.psum(loss_local, 'dp')]
    psum x1, waiting for transfers between devices: 53.8 us -> 106 us  [body(): flat = lax.psum(flat, 'dp')]
    all_gather x2 -> x1, blocking collectives: 76.9 us -> 40 us  [body(): every = lax.all_gather(jnp.concatenate(packs), 'dp')]
    convert_element_type x8 -> x4, local copies, waits for them, and re-layouts: 32.3 us -> 3.52 us  [low16(): return values.astype(jnp.bfloat16)]
    mul x0 -> x8, local copies, waits for them, and re-layouts: none -> 28.5 us  [the longest x4 14.5 us: token_backward(): d_scores.astype(jnp.float32).transpose(0, 2, 1)[..., None]]
    reduce_sum x6 -> x8, other arithmetic: 22.4 us -> 5.27 us  [layer_norm(): spread = jnp.mean(center * center, -1, keepdims=True)]
  transfers between devices with their start and end apart: 5 -> 4, of which waited for: 5 -> 4; matrix products, arithmetic and copies ran while one was open for 8% -> 5% of each run, Pallas kernels for 0% -> 0%
where the time goes in v1:
time: 782 us; the launch traced here: 776 us
  waiting for transfers between devices  331 us (42%)
  other arithmetic  171 us (22%)
  local copies, waits for them, and re-layouts  135 us (17%)
  blocking collectives  59.7 us (8%)
  matrix products  54 us (7%)
  between operations  25.4 us (3%)
    reduce_scatter x1, waiting for transfers between devices, body(): lax.psum_scatter(low16(table_full), 'dp', scatter_dimension=0, tiled=True)  138 us
    psum x1, waiting for transfers between devices, body(): flat = lax.psum(flat, 'dp')  106 us
    all_gather x1, waiting for transfers between devices, body(): wide = lax.all_gather(low16(word_table[0]), 'dp', axis=0, tiled=True)  72.8 us
    scatter-add x1, other arithmetic, body(): jax.ops.segment_sum(token_all, token_ids, num_segments=wide.shape[0])  58.1 us
    all_gather x1, blocking collectives, body(): every = lax.all_gather(jnp.concatenate(packs), 'dp')  40 us
    gather x2, local copies, waits for them, and re-layouts, body(): rows = jnp.take(wide, ids[enc], axis=0)  39.6 us
    unnamed x296, local copies, waits for them, and re-layouts  17.1 us
    unnamed x1, blocking collectives  16.3 us
  transfers between devices with their start and end apart: 4, of which 4 were waited for; matrix products, arithmetic and copies ran while one was open for 5% of the time, Pallas kernels for 0%

profile of v1, /device:TPU:0, one launch (start us, length us, event | category | flops | bytes accessed | tf_op | source)
XLA Modules:
  0.0 776.4 jit_solution(9468843921746077632)
XLA Ops:
  7.3 2.1 convert_element_type.289
  13.1 16.3 %all-reduce.3 = s32[1024]{0:T(1024)S(1)} all-reduce(s32[1024]{0:T(1024)S(1)} %add_dynamic-update-slice_fusion), channel_id=2, replica_groups=mesh['grp'=2,'dp'=16] {'dp'}, use_global_device_ids=true, to_apply=%add.3 | all-reduce | flops 1024 | bytes 8192
  49.6 72.8 %all-gather.5.cloned.1.call-done = bf16[1,30720,128]{2,1,0:T(8,128)(2,1)} async-done(((bf16[1,1920,128]{2,1,0:T(8,128)(2,1)}), bf16[1,30720,128]{2,1,0:T(8,128)(2,1)}) %all-gather.5.cloned.1.call-update) | async-done | bytes 7864336 | tf_op jit(solution)/shard_map/all_gather | solution.py:235
  122.4 7.4 gather_fusion
  129.8 32.2 %gather_fusion.1 = bf16[8192,128]{1,0:T(8,128)(2,1)} fusion(bf16[30720,128]{1,0:T(8,128)(2,1)} %bitcast.322, s32[8192]{0:T(1024)S(1)} %broadcast_clamp_fusion), kind=kCustom, calls=%fused_computation.1 | custom fusion | bytes 4227072 | tf_op jit(solution)/shard_map/jit(_take)/gather | solution.py:248
  163.5 4.1 fusion.12
  168.3 2.3 multiply_reduce_fusion.2
  176.5 3.2 reshape.1107
  179.7 3.4 slice_bitcast_fusion.7
  183.2 2.0 copy.164
  185.1 2.0 fusion.77
  193.4 3.2 add_convert_fusion.1
  198.9 2.9 add_convert_fusion
  205.0 2.2 fusion.19
  207.4 40.0 %all-gather.2 = bf16[768,256]{1,0:T(8,128)(2,1)S(1)} all-gather(bf16[48,256]{1,0:T(8,128)(2,1)S(1)} %maximum_maximum_fusion), channel_id=4, replica_groups=mesh['grp'=2,'dp'=16] {'dp'}, dimensions={0}, use_global_device_ids=true | all-gather | bytes 417792 | tf_op jit(solution)/shard_map/all_gather | solution.py:254
  249.3 3.5 mul.1284
  252.8 2.6 mul.1285
  281.2 2.0 fusion.18
  284.9 2.2 fusion.16
  289.9 2.2 convert_reduce_fusion.2
  292.1 2.0 multiply_reduce_fusion.18
  308.4 3.1 mul.1278
  311.5 2.6 mul.1279
  323.0 2.7 fusion.179
  325.7 3.1 mul.1325
  328.8 5.6 copy.130
  334.4 2.3 mul.1331
  336.7 5.6 copy.131
  342.3 5.6 convert_reduce_fusion
  350.0 1.9 copy-done
  353.7 4.1 multiply_reduce_fusion.1
  357.8 5.7 multiply_reduce_fusion
  363.5 7.1 fusion.178
  370.6 58.1 %scatter_custom_fusion = f32[30720,128]{1,0:T(8,128)} fusion(s32[9216]{0:T(1024)} %pad_add_fusion, f32[]{:T(128)} %constant.261.clone.1, f32[8192,128]{1,0:T(8,128)} %bitcast.323, f32[]{:T(128)} %constant.265.clone.1, f32[1024,128]{1,0:T(8,128)S(1)} %bitcast.331), kind=kCustom, calls=%fused_computation.10 | custom fusion | flops 2359296 | bytes 20448256 | tf_op jit(solution)/shard_map/scatter-add | solution.py:290
  428.8 8.5 %convert_element_type.351 = bf16[30720,128]{1,0:T(8,128)(2,1)} convert(f32[30720,128]{1,0:T(8,128)} %scatter_custom_fusion) | non-fusion elementwise | flops 3932160 | bytes 23592960 | tf_op jit(solution)/shard_map/convert_element_type | solution.py:35
  441.5 3.1 fusion.26
  450.8 138.5 %reduce-scatter.2.cloned.1.call-done = bf16[1920,128]{1,0:T(8,128)(2,1)} async-done(((bf16[30720,128]{1,0:T(8,128)(2,1)}), bf16[1920,128]{1,0:T(8,128)(2,1)}) %reduce-scatter.2.cloned.1.call-update) | async-done | bytes 491536 | tf_op jit(solution)/shard_map/reduce_scatter | solution.py:291
  591.2 9.5 %concatenate.141 = f32[164865]{0:T(1024)} concatenate(f32[1]{0:T(128)} %bitcast.79, f32[32768]{0:T(1024)S(1)} %pad_bitcast_fusion, f32[49152]{0:T(1024)S(1)} %copy-done.50, f32[512]{0:T(512)S(1)} %maximum_bitcast_fusion.4, f32[32768]{0:T(1024)S(1)} %bitcast.349, f32[49152]{0:T(1024)S(1)} %reshape.1128, f32[512]{0:T(512)S(1)} %maximum_bitcast_fusion.5), dimensions={0} | concatenate | bytes 1318920 | tf_op jit(solution)/shard_map/concatenate | solution.py:295
  603.9 105.9 %all-reduce.8.cloned.1.call-done = f32[164865]{0:T(1024)} async-done(((f32[164865]{0:T(1024)}), f32[164865]{0:T(1024)}) %all-reduce.8.cloned.1.call-update) | async-done | bytes 659476 | tf_op jit(solution)/shard_map/psum | solution.py:298
  724.4 2.4 bitcast_subtract_fusion.3
  726.8 3.0 bitcast_subtract_fusion.2
  729.9 2.3 bitcast_subtract_fusion
  733.3 2.1 bitcast_subtract_fusion.1
  738.8 3.4 psum.47
  744.1 13.7 %all-reduce.10.cloned.1.call-done = (f32[1920,128]{1,0:T(8,128)}, f32[2,256,128]{2,1,0:T(8,128)}, f32[2,128,512]{2,1,0:T(8,128)}, f32[2,2,128,512]{3,2,1,0:T(8,128)}) async-done(((f32[1920,128]{1,0:T(8,128)}, f32[2,256,128]{2,1,0:T(8,128)}, f32[2,128,512]{2,1,0:T(8,128)}, f32[2,2,128,512]{3,2,1,0:T(8,128)}), (f32[1920,128]{1,0:T(8,128)}, f32[2,256,128]{2,1,0:T(8,128)}, f32[2,128,512]{2,1,0:T(8,128)}, ...) | async-done | bytes 2818064 | tf_op jit(solution)/shard_map/psum | solution.py:332
  757.7 2.0 subtract_bitcast_fusion.3
  759.8 2.7 subtract_bitcast_fusion.2
  764.3 2.0 subtract_bitcast_fusion
  (495 shorter events, 133.5 us)
Async XLA Ops:
  7.2 41.7 %copy-start.63 = (s32[16,64]{1,0:T(8,128)S(1)}, s32[16,64]{1,0:T(8,128)}, u32[]{:S(2)}) copy-start(s32[16,64]{1,0:T(8,128)} %param.36) | copy-start | bytes 12292
  7.2 41.7 %copy-start.54 = (s32[32,256]{1,0:T(8,128)S(1)}, s32[32,256]{1,0:T(8,128)}, u32[]{:S(2)}) copy-start(s32[32,256]{1,0:T(8,128)} %param.37) | copy-start | bytes 98308
  7.2 33.4 %copy-start.7 = (f32[1,2,2,128,512]{4,3,2,1,0:T(8,128)S(1)}, f32[1,2,2,128,512]{4,3,2,1,0:T(8,128)}, u32[]{:S(2)}) copy-start(f32[1,2,2,128,512]{4,3,2,1,0:T(8,128)} %param.46) | copy-start | bytes 3145732
  7.2 38.4 %copy-start.139 = (s32[16]{0:T(128)S(1)}, s32[16]{0:T(128)}, u32[]{:S(2)}) copy-start(s32[16]{0:T(128)} %param.38) | copy-start | bytes 196
  7.2 39.0 %copy-start.51 = (f32[1,2,256,128]{3,2,1,0:T(8,128)S(1)}, f32[1,2,256,128]{3,2,1,0:T(8,128)}, u32[]{:S(2)}) copy-start(f32[1,2,256,128]{3,2,1,0:T(8,128)} %param.44) | copy-start | bytes 786436
  7.3 41.0 %copy-start.140 = (s32[32]{0:T(128)S(1)}, s32[32]{0:T(128)}, u32[]{:S(2)}) copy-start(s32[32]{0:T(128)} %param.39) | copy-start | bytes 388
  7.3 115.1 %all-gather.5.cloned.1.call-start = ((), (), s32[]{:S(2)}) async-start(), calls=%async_computation.3 | async-start | bytes 8355840 | tf_op jit(solution)/shard_map/all_gather | solution.py:235
  9.5 579.8 %reduce-scatter.2.cloned.1.call-start = ((), (), s32[]{:S(2)}) async-start(), calls=%async_computation.1 | async-start | bytes 8355840 | tf_op jit(solution)/shard_map/reduce_scatter | solution.py:291
  40.7 158.3 %copy-start.42 = (bf16[1,1,128,512]{2,3,1,0:T(8,128)(2,1)}, bf16[1,1,128,512]{2,3,1,0:T(8,128)(2,1)S(1)}, u32[]{:S(2)}) copy-start(bf16[1,1,128,512]{2,3,1,0:T(8,128)(2,1)S(1)} %copy.185) | copy-start | bytes 393220
  40.7 221.1 %copy-start.19 = (bf16[1,2,2,128,512]{4,3,2,1,0:T(8,128)(2,1)}, bf16[1,2,2,128,512]{4,3,2,1,0:T(8,128)(2,1)S(1)}, u32[]{:S(2)}) copy-start(bf16[1,2,2,128,512]{4,3,2,1,0:T(8,128)(2,1)S(1)} %convert.26) | copy-start | bytes 1572868
  171.0 25.6 %copy-start.29 = (bf16[16,64,128]{2,1,0:T(8,128)(2,1)}, bf16[16,64,128]{2,1,0:T(8,128)(2,1)S(1)}, u32[]{:S(2)}) copy-start(bf16[16,64,128]{2,1,0:T(8,128)(2,1)S(1)} %add_convert_fusion.2) | copy-start | bytes 786436
  204.4 43.1 %copy-start.71 = (f32[32,2,256]{2,1,0:T(2,128)}, f32[32,2,256]{2,1,0:T(2,128)S(1)}, u32[]{:S(2)}) copy-start(f32[32,2,256]{2,1,0:T(2,128)S(1)} %fusion.29) | copy-start | bytes 196612
  247.5 12.7 %copy-start.24 = (bf16[16,32,256]{2,1,0:T(8,128)(2,1)}, bf16[16,32,256]{2,1,0:T(8,128)(2,1)S(1)}, u32[]{:S(2)}) copy-start(bf16[16,32,256]{2,1,0:T(8,128)(2,1)S(1)} %slice.440) | copy-start | bytes 786436
  261.6 16.8 %copy-start.60 = (f32[512]{0:T(512)}, f32[512]{0:T(512)S(1)}, u32[]{:S(2)}) copy-start(f32[512]{0:T(512)S(1)} %broadcast_multiply_fusion.8) | copy-start | bytes 6148
  261.9 16.6 %copy-start.76 = (f32[512]{0:T(512)}, f32[512]{0:T(512)S(1)}, u32[]{:S(2)}) copy-start(f32[512]{0:T(512)S(1)} %fusion.147) | copy-start | bytes 6148
  292.1 22.0 %copy-start.21 = (f32[16,64,128]{2,1,0:T(8,128)S(1)}, f32[16,64,128]{2,1,0:T(8,128)}, u32[]{:S(2)}) copy-start(f32[16,64,128]{2,1,0:T(8,128)} %mul.1285) | copy-start | bytes 1572868
  437.3 272.4 %all-reduce.8.cloned.1.call-start = ((), (), s32[]{:S(2)}) async-start(), calls=%async_computation.2 | async-start | bytes 1327104 | tf_op jit(solution)/shard_map/psum | solution.py:298
  444.6 146.6 %copy-start.50 = (f32[49152]{0:T(1024)S(1)}, f32[49152]{0:T(1024)}, u32[]{:S(2)}) copy-start(f32[49152]{0:T(1024)} %reshape.1125) | copy-start | bytes 589828
  444.6 146.6 %copy-start.52 = (f32[256,128]{1,0:T(8,128)S(1)}, f32[256,128]{1,0:T(8,128)}, u32[]{:S(2)}) copy-start(f32[256,128]{1,0:T(8,128)} %get-tuple-element.203) | copy-start | bytes 393220
  444.7 156.2 %copy-start.34 = (bf16[256,512]{1,0:T(8,128)(2,1)S(1)}, bf16[256,512]{1,0:T(8,128)(2,1)}, u32[]{:S(2)}) copy-start(bf16[256,512]{1,0:T(8,128)(2,1)} %copy-done.33) | copy-start | bytes 786436
  444.7 156.2 %copy-start.79 = (f32[256]{0:T(256)S(1)}, f32[256]{0:T(256)}, u32[]{:S(2)}) copy-start(f32[256]{0:T(256)} %copy-done.78) | copy-start | bytes 3076
  444.7 156.2 %copy-start.85 = (f32[256]{0:T(256)S(1)}, f32[256]{0:T(256)}, u32[]{:S(2)}) copy-start(f32[256]{0:T(256)} %copy-done.84) | copy-start | bytes 3076
  444.7 156.2 %copy-start.97 = (f32[128]{0:T(128)S(1)}, f32[128]{0:T(128)}, u32[]{:S(2)}) copy-start(f32[128]{0:T(128)} %get-tuple-element.259) | copy-start | bytes 1540
  444.7 156.2 %copy-start.109 = (f32[128]{0:T(128)S(1)}, f32[128]{0:T(128)}, u32[]{:S(2)}) copy-start(f32[128]{0:T(128)} %get-tuple-element.258) | copy-start | bytes 1540
  448.8 153.4 %copy-start.27 = (f32[256,128]{1,0:T(8,128)S(1)}, f32[256,128]{1,0:T(8,128)}, u32[]{:S(2)}) copy-start(f32[256,128]{1,0:T(8,128)} %copy-done.26) | copy-start | bytes 393220
  448.8 153.4 %copy-start.49 = (bf16[16,16,256]{2,1,0:T(8,128)(2,1)S(1)}, bf16[16,16,256]{2,1,0:T(8,128)(2,1)}, u32[]{:S(2)}) copy-start(bf16[16,16,256]{2,1,0:T(8,128)(2,1)} %copy-done.48) | copy-start | bytes 393220
  448.8 154.2 %copy-start.25 = (bf16[16,32,256]{2,1,0:T(8,128)(2,1)S(1)}, bf16[16,32,256]{2,1,0:T(8,128)(2,1)}, u32[]{:S(2)}) copy-start(bf16[16,32,256]{2,1,0:T(8,128)(2,1)} %copy-done.24) | copy-start | bytes 786436
  450.7 262.5 %copy-start.124 = (f32[128]{0:T(128)S(1)}, f32[128]{0:T(128)}, u32[]{:S(2)}) copy-start(f32[128]{0:T(128)} %get-tuple-element.191) | copy-start | bytes 1540
  450.7 262.4 %copy-start.125 = (f32[128]{0:T(128)S(1)}, f32[128]{0:T(128)}, u32[]{:S(2)}) copy-start(f32[128]{0:T(128)} %get-tuple-element.193) | copy-start | bytes 1540
  450.8 262.4 %copy-start.131 = (f32[512]{0:T(512)S(1)}, f32[512]{0:T(512)}, u32[]{:S(2)}) copy-start(f32[512]{0:T(512)} %get-tuple-element.295) | copy-start | bytes 6148
  450.8 262.4 %copy-start.132 = (f32[128]{0:T(128)S(1)}, f32[128]{0:T(128)}, u32[]{:S(2)}) copy-start(f32[128]{0:T(128)} %get-tuple-element.152) | copy-start | bytes 1540
  450.8 262.4 %copy-start.133 = (f32[128]{0:T(128)S(1)}, f32[128]{0:T(128)}, u32[]{:S(2)}) copy-start(f32[128]{0:T(128)} %get-tuple-element.158) | copy-start | bytes 1540
  450.8 262.4 %copy-start.134 = (f32[128]{0:T(128)S(1)}, f32[128]{0:T(128)}, u32[]{:S(2)}) copy-start(f32[128]{0:T(128)} %get-tuple-element.154) | copy-start | bytes 1540
  450.8 262.4 %copy-start.135 = (f32[128]{0:T(128)S(1)}, f32[128]{0:T(128)}, u32[]{:S(2)}) copy-start(f32[128]{0:T(128)} %get-tuple-element.159) | copy-start | bytes 1540
  591.2 122.1 %copy-start.118 = (f32[128]{0:T(128)S(1)}, f32[128]{0:T(128)}, u32[]{:S(2)}) copy-start(f32[128]{0:T(128)} %get-tuple-element.145) | copy-start | bytes 1540
  591.2 122.1 %copy-start.119 = (f32[128]{0:T(128)S(1)}, f32[128]{0:T(128)}, u32[]{:S(2)}) copy-start(f32[128]{0:T(128)} %get-tuple-element.156) | copy-start | bytes 1540
  591.2 122.1 %copy-start.120 = (f32[128]{0:T(128)S(1)}, f32[128]{0:T(128)}, u32[]{:S(2)}) copy-start(f32[128]{0:T(128)} %get-tuple-element.195) | copy-start | bytes 1540
  591.2 122.1 %copy-start.121 = (f32[128]{0:T(128)S(1)}, f32[128]{0:T(128)}, u32[]{:S(2)}) copy-start(f32[128]{0:T(128)} %get-tuple-element.147) | copy-start | bytes 1540
  591.2 122.1 %copy-start.122 = (f32[128]{0:T(128)S(1)}, f32[128]{0:T(128)}, u32[]{:S(2)}) copy-start(f32[128]{0:T(128)} %get-tuple-element.157) | copy-start | bytes 1540
  591.2 122.1 %copy-start.123 = (f32[128]{0:T(128)S(1)}, f32[128]{0:T(128)}, u32[]{:S(2)}) copy-start(f32[128]{0:T(128)} %get-tuple-element.197) | copy-start | bytes 1540
  591.2 122.1 %copy-start.130 = (f32[512]{0:T(512)S(1)}, f32[512]{0:T(512)}, u32[]{:S(2)}) copy-start(f32[512]{0:T(512)} %get-tuple-element.293) | copy-start | bytes 6148
  600.8 156.9 %all-reduce.10.cloned.1.call-start = ((), (), s32[]{:S(2)}) async-start(), calls=%async_computation.4 | async-start | bytes 5636096 | tf_op jit(solution)/shard_map/psum | solution.py:332
  715.1 14.7 %copy-start.8 = (f32[1,2,2,128,512]{4,3,2,1,0:T(8,128)S(1)}, f32[1,2,2,128,512]{4,3,2,1,0:T(8,128)}, u32[]{:S(2)}) copy-start(f32[1,2,2,128,512]{4,3,2,1,0:T(8,128)} %param.46) | copy-start | bytes 3145732
  715.1 14.7 %copy-start.9 = (f32[2,2,128,512]{3,2,1,0:T(8,128)S(1)}, f32[2,2,128,512]{3,2,1,0:T(8,128)}, u32[]{:S(2)}) copy-start(f32[2,2,128,512]{3,2,1,0:T(8,128)} %param.61) | copy-start | bytes 3145732
  733.3 24.4 %copy-start.36 = (f32[2,256,128]{2,1,0:T(8,128)S(1)}, f32[2,256,128]{2,1,0:T(8,128)}, u32[]{:S(2)}) copy-start(f32[2,256,128]{2,1,0:T(8,128)} %param.59) | copy-start | bytes 786436
  733.3 24.4 %copy-start.56 = (f32[2,256,128]{2,1,0:T(8,128)S(1)}, f32[2,256,128]{2,1,0:T(8,128)}, u32[]{:S(2)}) copy-start(f32[2,256,128]{2,1,0:T(8,128)} %param.64) | copy-start | bytes 786436
  735.4 24.3 %copy-start.22 = (f32[2,128,512]{2,1,0:T(8,128)S(1)}, f32[2,128,512]{2,1,0:T(8,128)}, u32[]{:S(2)}) copy-start(f32[2,128,512]{2,1,0:T(8,128)} %param.60) | copy-start | bytes 1572868
  735.4 27.0 %copy-start.12 = (f32[1920,128]{1,0:T(8,128)S(1)}, f32[1920,128]{1,0:T(8,128)}, u32[]{:S(2)}) copy-start(f32[1920,128]{1,0:T(8,128)} %param.58) | copy-start | bytes 2949124
  (98 other events, 477.7 us)
Sparse Core Ops, SparseCore 0:
  11.5 110.8 all-gather.4
  437.5 151.7 reduce-scatter.1
  600.9 108.8 all-reduce.7
  735.6 22.0 all-reduce.9
